TPU v7x, 32 devices: a whole 2x2x4 slice. The times are simulated.
32 devices in a mesh: groups: 2 (over y), ctx: 4 (over z), head: 2 (over x), row: 2 (over core).
Axes of the slice: x: 2, y: 2, z: 4, core: 2. Of those that a mesh axis runs over, the one named last changes fastest.
Arguments:
- queries: bfloat16 [512, 4, 8192], P(('groups', 'ctx', 'row'), None, 'head'), parts along dimension 0, may hold values from -128 to 128
- row_new_keys: bfloat16 [512, 4, 1024], P(('groups', 'ctx', 'row'), None, 'head'), parts along dimension 0, may hold values from -4 to 4
- row_new_values: bfloat16 [512, 4, 1024], P(('groups', 'ctx', 'row'), None, 'head'), parts along dimension 0, may hold values from -6 to 6
- prefix_page_keys: bfloat16 [4096, 1024], P(('groups', 'ctx'), 'head'), parts along dimension 0, may hold values from -6 to 6
- prefix_page_values: bfloat16 [4096, 1024], P(('groups', 'ctx'), 'head'), parts along dimension 0, may hold values from -6 to 6
- block_pages: int32 [64, 8], P('groups'), parts along dimension 0, may hold values from 0 to 15, as said below
- row_len: int32 [512], P(('groups', 'ctx', 'row')), parts along dimension 0, may hold values from 1 to 8
- home: int32 [512, 1], P(('groups', 'ctx', 'row')), parts along dimension 0, may hold values from 0 to 7; in each aligned block of 32 rows (0 to 31, 32 to 63, ...) at most 8 rows name the same one
Outputs:
- delivered: bfloat16 [16, 8, 8, 4, 8192], P(('groups', 'ctx', 'row'), None, None, None, 'head'), parts along dimension 0
There are 2 independent parts, one for each index of `groups`. A program takes and returns all parts, laid end to end along the dimension named above; each array names one. Nothing has to cross between parts.
Inputs may be any that keep to these rules, and one draw needn't show every extreme that they name: `block_pages`: each row block's entries are distinct pages; blocks 2i and 2i + 1 share their first half of entries. `home`: among the 32 rows of one device, at most 8 name the same owner.
All inputs are finite; a program needn't handle non-finite values.
Results may differ from a plain program's by a relative error of at most 0.0055.
Values may be sent and summed in bfloat16 or wider, within the bound.
A program may use at most 64 MiB of HBM per device.

v0:
```python
import jax
import jax.numpy as jnp
from jax import lax
from jax.sharding import PartitionSpec as P

HEAD_SIZE = 128
PAGE_TOKENS = 128
BLOCK_ROWS = 8


LOWEST = -1e30


def causal_state(grouped_heads, fresh_keys, fresh_values, factor):
    scores = (
        jnp.einsum(
            "rtjgd,rujd->rtjgu", grouped_heads, fresh_keys, preferred_element_type=jnp.float32
        )
        * factor
    )
    length = grouped_heads.shape[1]
    allowed = (jnp.arange(length)[None, :] <= jnp.arange(length)[:, None])[None, :, None, None, :]
    maxima = jnp.max(jnp.where(allowed, scores, LOWEST), axis=-1)
    weights = jnp.where(allowed, jnp.exp(scores - maxima[..., None]), 0.0)
    totals = jnp.sum(weights, axis=-1)
    weighted = jnp.einsum(
        "rtjgu,rujd->rtjgd",
        weights.astype(jnp.bfloat16),
        fresh_values,
        preferred_element_type=jnp.float32,
    )
    return (maxima, totals, weighted)


def page_usage(global_rows, lengths, block_pages, prefix_pool_pages):
    block_count = block_pages.shape[0]
    slot_count = block_pages.shape[1]
    owner_block = (global_rows[:, None] // BLOCK_ROWS == jnp.arange(block_count)[None, :]).astype(
        jnp.float32
    )
    page_marks = (block_pages[:, :, None] == jnp.arange(prefix_pool_pages)[None, None, :]).astype(
        jnp.float32
    )
    picked = jnp.dot(
        owner_block,
        page_marks.reshape(block_count, slot_count * prefix_pool_pages),
        precision=lax.Precision.HIGHEST,
    ).reshape(-1, slot_count, prefix_pool_pages)
    live_slots = (jnp.arange(slot_count)[None, :] < lengths[:, None]).astype(jnp.float32)
    return jnp.sum(picked * live_slots[:, :, None], axis=1) > 0.5


def attend_block(carried, grouped_heads, mask_pages, keys_blk, values_blk, factor):
    maxima, totals, weighted = carried
    scores = (
        jnp.einsum("rtjgd,njd->rtjgn", grouped_heads, keys_blk, preferred_element_type=jnp.float32)
        * factor
    )
    mask_tokens = jnp.repeat(mask_pages, PAGE_TOKENS, axis=1)[:, None, None, None, :]
    raised = jnp.maximum(maxima, jnp.max(jnp.where(mask_tokens, scores, LOWEST), axis=-1))
    weights = jnp.where(mask_tokens, jnp.exp(scores - raised[..., None]), 0.0)
    retain = jnp.exp(maxima - raised)
    totals = totals * retain + jnp.sum(weights, axis=-1)
    weighted = weighted * retain[..., None] + jnp.einsum(
        "rtjgn,njd->rtjgd",
        weights.astype(jnp.bfloat16),
        values_blk,
        preferred_element_type=jnp.float32,
    )
    return (raised, totals, weighted)


def fold_pages(running, grouped_heads, used_pages, page_k, page_v, factor):
    token_count = page_k.shape[0]
    block_len = PAGE_TOKENS * max(1, 512 // PAGE_TOKENS)
    kv_local = page_k.shape[1] // HEAD_SIZE

    def advance(number, carried):
        offset = number * block_len
        keys_blk = lax.dynamic_slice_in_dim(page_k, offset, block_len, 0).reshape(
            block_len, kv_local, HEAD_SIZE
        )
        values_blk = lax.dynamic_slice_in_dim(page_v, offset, block_len, 0).reshape(
            block_len, kv_local, HEAD_SIZE
        )
        mask_pages = lax.dynamic_slice_in_dim(
            used_pages, offset // PAGE_TOKENS, block_len // PAGE_TOKENS, 1
        )
        return lax.cond(
            jnp.any(mask_pages),
            lambda current: attend_block(
                current, grouped_heads, mask_pages, keys_blk, values_blk, factor
            ),
            lambda current: current,
            carried,
        )

    return lax.fori_loop(0, token_count // block_len, advance, running)


def body(
    queries,
    row_new_keys,
    row_new_values,
    prefix_page_keys,
    prefix_page_values,
    block_pages,
    row_len,
    home,
):
    local_rows = queries.shape[0]
    step_count = queries.shape[1]
    row_width = queries.shape[2]
    kv_local = row_new_keys.shape[2] // HEAD_SIZE
    group_size = row_width // row_new_keys.shape[2]
    factor = HEAD_SIZE ** (-0.5)
    ctx_count = lax.axis_size("ctx")
    row_count = lax.axis_size("row")
    prefix_pool_pages = prefix_page_keys.shape[0] * ctx_count // PAGE_TOKENS
    grouped_heads = queries.reshape(local_rows, step_count, kv_local, group_size, HEAD_SIZE)
    fresh_keys = row_new_keys.reshape(local_rows, step_count, kv_local, HEAD_SIZE)
    fresh_values = row_new_values.reshape(local_rows, step_count, kv_local, HEAD_SIZE)
    own_max, own_total, own_weighted = causal_state(grouped_heads, fresh_keys, fresh_values, factor)
    row_start = lax.axis_index(("ctx", "row")) * local_rows
    used_pages = page_usage(
        row_start + jnp.arange(local_rows), row_len, block_pages, prefix_pool_pages
    )
    maxima, totals, weighted = fold_pages(
        (own_max, own_total, own_weighted),
        grouped_heads,
        used_pages,
        lax.all_gather(prefix_page_keys, "ctx", axis=0, tiled=True),
        lax.all_gather(prefix_page_values, "ctx", axis=0, tiled=True),
        factor,
    )
    attended = (
        (weighted / totals[..., None])
        .astype(jnp.bfloat16)
        .reshape(local_rows, step_count * row_width)
    )
    owner_count = ctx_count * row_count
    capacity = max(2, 2 * local_rows // owner_count)
    targets = home[:, 0]
    row_order = jnp.arange(local_rows)
    earlier = (targets[:, None] == targets[None, :]) & (row_order[:, None] > row_order[None, :])
    position = jnp.sum(earlier.astype(jnp.int32), axis=1)
    slot_ids = targets * capacity + position
    placing = (jnp.arange(owner_count * capacity)[:, None] == slot_ids[None, :]).astype(
        jnp.bfloat16
    )
    outgoing = jnp.dot(placing, attended, preferred_element_type=jnp.float32).astype(jnp.bfloat16)
    outbox = outgoing.reshape(owner_count, capacity, step_count, row_width)
    arrived = lax.all_to_all(outbox, ("ctx", "row"), split_axis=0, concat_axis=0, tiled=True)
    return arrived.reshape(1, owner_count, capacity, step_count, row_width)


def solution(mesh):
    return jax.shard_map(
        body,
        mesh=mesh,
        in_specs=(
            P(("groups", "ctx", "row"), None, "head"),
            P(("groups", "ctx", "row"), None, "head"),
            P(("groups", "ctx", "row"), None, "head"),
            P(("groups", "ctx"), "head"),
            P(("groups", "ctx"), "head"),
            P("groups", None),
            P(("groups", "ctx", "row")),
            P(("groups", "ctx", "row"), None),
        ),
        out_specs=P(("groups", "ctx", "row"), None, None, None, "head"),
        check_vma=False,
    )
```

profile of v0, /device:TPU:0, one launch (start us, length us, event | category | flops | bytes accessed | tf_op | source)
XLA Modules:
  0.0 228.4 jit_solution(5961262684706914406)
XLA Ops:
  6.5 2.1 copy.60
  8.8 2.0 copy.61
  10.9 1.1 reshape.145
  12.0 0.7 copy.66
  12.7 5.5 %select_reduce_fusion = (f32[32,4,4,8]{3,1,2,0:T(4,128)}, f32[32,4,4,8,4]{3,4,1,2,0:T(4,128)S(1)}) fusion(pred[4,4]{1,0:T(4,128)(4,1)S(1)} %iota_compare_fusion.5, bf16[32,4,4,8,128]{4,3,2,1,0:T(8,128)(2,1)S(1)} %reshape.145, bf16[32,4,512]{2,1,0:T(4,128)(2,1)S(1)} %copy-done.5), kind=kOutput, calls=%fused_computation.27 | convolution fusion | flops 4239360 | bytes 1261584 | tf_op jit(solution)/shard_map/rtjgd,rujd->rtjgu/dot_general | solution.py:16
  18.2 1.1 copy.62
  19.3 1.7 convolution_bitcast_fusion
  21.0 1.5 copy.64
  22.5 1.0 fusion.15
  23.5 0.2 copy.63
  23.9 0.2 convert_reduce_fusion
  24.1 0.2 fusion.10
  24.3 33.3 %all-gather.3.cloned.1.call-done = bf16[2048,512]{0,1:T(8,128)(2,1)} async-done(((bf16[512,512]{0,1:T(8,128)(2,1)}), bf16[2048,512]{0,1:T(8,128)(2,1)}) %all-gather.3.cloned.1.call-update) | async-done | bytes 2097168 | tf_op jit(solution)/shard_map/all_gather | solution.py:132
  57.6 46.3 %all-gather.5.cloned.1.call-done = bf16[2048,512]{0,1:T(8,128)(2,1)} async-done(((bf16[512,512]{0,1:T(8,128)(2,1)}), bf16[2048,512]{0,1:T(8,128)(2,1)}) %all-gather.5.cloned.1.call-update) | async-done | bytes 2097168 | tf_op jit(solution)/shard_map/all_gather | solution.py:133
  103.9 60.1 %while.19 = (s32[]{:T(128)}, f32[32,4,4,8]{0,3,1,2:T(8,128)S(1)}, f32[32,4,4,8]{0,3,1,2:T(8,128)S(1)}, f32[32,4,4,8,128]{4,3,1,0,2:T(8,128)}, pred[32,16]{0,1:T(...) while((s32[]{:T(128)}, f32[32,4,4,8]{0,3,1,2:T(8,128)S(1)}, ...), condition=%wide.region_10.11_spmd, body=%wide.region_4.10_spmd.sunk | while | flops 1091575936 | bytes 33916024 | solution.py:98
  103.9 0.7 fusion.35
  105.3 13.6 %conditional.2 = ((f32[32,4,4,8]{0,3,1,2:T(8,128)S(1)}, f32[32,4,4,8]{0,3,1,2:T(8,128)S(1)}, f32[32,4,4,8,128]{4,3,1,0,2:T(8,128)})) conditional(s32[]{:T(128)} %convert_element_type.51, (f32[32,4,4,8]{0,3,1,2:T(8,128)S(1)}, f32[32,4,4,8]{0,3,1,2:T(8,128)S(1)}, f32[32,4,4,8,128]{4,3,1,0,2:T(8,128)}) %tuple.66, (pred[32,4]{1,0:T(8,128)(4,1)S(1)}, ...), branch_computations={%region_6.6_spmd, %region_7.9_spmd} | conditional | flops 1091575808 | bytes 33915068 | solution.py:89
  105.3 1.3 constant_dynamic-slice_fusion
  106.7 1.3 fusion
  108.1 3.7 %fusion.3 = (bf16[32,4,4,8,512]{4,0,3,1,2:T(8,128)(2,1)}, f32[32,4,4,8]{0,3,1,2:T(8,128)S(1)}) fusion(f32[4,512,32,4,8]{1,2,4,3,0:T(8,128)S(1)} %get-tuple-element.380, f32[32,4,4,8]{0,3,1,2:T(8,128)S(1)} %max.5, pred[32,512]{1,0:T(8,128)(4,1)S(1)} %bitcast.76), kind=kLoop, calls=%fused_computation.5 | loop fusion | flops 10481664 | bytes 12632064 | tf_op jit(solution)/shard_map/while/body/eval_jaxpr/cond/branch_1_fun/convert_element_type | solution.py:66
  111.9 0.1 copy.53
  112.0 6.9 %bitcast_add_fusion = f32[32,4,4,8,128]{4,3,1,0,2:T(8,128)} fusion(f32[32,4,4,8,128]{4,3,1,0,2:T(8,128)} %get-tuple-element.307, bf16[512,4,128,1,1]{0,2,4,3,1:T(8,128)(2,1)S(1)} %bitcast.71, bf16[32,4,4,8,512]{4,0,3,1,2:T(8,128)(2,1)} %get-tuple-element.377, f32[32,4,4,8]{3,1,0,2:T(4,128)S(1)} %copy.53), kind=kOutput, calls=%fused_computation.9 | convolution fusion | flops 537919488 | bytes 8929280 | tf_op jit(solution)/shard_map/while/body/eval_jaxpr/cond/branch_1_fun/rtjgn,njd->rtjgd/dot_general | solution.py:64
  118.9 0.7 fusion.35
  120.3 13.6 %conditional.2 = ((f32[32,4,4,8]{0,3,1,2:T(8,128)S(1)}, f32[32,4,4,8]{0,3,1,2:T(8,128)S(1)}, f32[32,4,4,8,128]{4,3,1,0,2:T(8,128)})) conditional(s32[]{:T(128)} %convert_element_type.51, (f32[32,4,4,8]{0,3,1,2:T(8,128)S(1)}, f32[32,4,4,8]{0,3,1,2:T(8,128)S(1)}, f32[32,4,4,8,128]{4,3,1,0,2:T(8,128)}) %tuple.66, (pred[32,4]{1,0:T(8,128)(4,1)S(1)}, ...), branch_computations={%region_6.6_spmd, %region_7.9_spmd} | conditional | flops 1091575808 | bytes 33915068 | solution.py:89
  120.3 1.3 constant_dynamic-slice_fusion
  121.7 1.3 fusion
  123.1 3.7 %fusion.3 = (bf16[32,4,4,8,512]{4,0,3,1,2:T(8,128)(2,1)}, f32[32,4,4,8]{0,3,1,2:T(8,128)S(1)}) fusion(f32[4,512,32,4,8]{1,2,4,3,0:T(8,128)S(1)} %get-tuple-element.380, f32[32,4,4,8]{0,3,1,2:T(8,128)S(1)} %max.5, pred[32,512]{1,0:T(8,128)(4,1)S(1)} %bitcast.76), kind=kLoop, calls=%fused_computation.5 | loop fusion | flops 10481664 | bytes 12632064 | tf_op jit(solution)/shard_map/while/body/eval_jaxpr/cond/branch_1_fun/convert_element_type | solution.py:66
  126.9 0.1 copy.53
  127.0 6.9 %bitcast_add_fusion = f32[32,4,4,8,128]{4,3,1,0,2:T(8,128)} fusion(f32[32,4,4,8,128]{4,3,1,0,2:T(8,128)} %get-tuple-element.307, bf16[512,4,128,1,1]{0,2,4,3,1:T(8,128)(2,1)S(1)} %bitcast.71, bf16[32,4,4,8,512]{4,0,3,1,2:T(8,128)(2,1)} %get-tuple-element.377, f32[32,4,4,8]{3,1,0,2:T(4,128)S(1)} %copy.53), kind=kOutput, calls=%fused_computation.9 | convolution fusion | flops 537919488 | bytes 8929280 | tf_op jit(solution)/shard_map/while/body/eval_jaxpr/cond/branch_1_fun/rtjgn,njd->rtjgd/dot_general | solution.py:64
  133.9 0.7 fusion.35
  135.3 13.6 %conditional.2 = ((f32[32,4,4,8]{0,3,1,2:T(8,128)S(1)}, f32[32,4,4,8]{0,3,1,2:T(8,128)S(1)}, f32[32,4,4,8,128]{4,3,1,0,2:T(8,128)})) conditional(s32[]{:T(128)} %convert_element_type.51, (f32[32,4,4,8]{0,3,1,2:T(8,128)S(1)}, f32[32,4,4,8]{0,3,1,2:T(8,128)S(1)}, f32[32,4,4,8,128]{4,3,1,0,2:T(8,128)}) %tuple.66, (pred[32,4]{1,0:T(8,128)(4,1)S(1)}, ...), branch_computations={%region_6.6_spmd, %region_7.9_spmd} | conditional | flops 1091575808 | bytes 33915068 | solution.py:89
  135.4 1.3 constant_dynamic-slice_fusion
  136.8 1.3 fusion
  138.1 3.7 %fusion.3 = (bf16[32,4,4,8,512]{4,0,3,1,2:T(8,128)(2,1)}, f32[32,4,4,8]{0,3,1,2:T(8,128)S(1)}) fusion(f32[4,512,32,4,8]{1,2,4,3,0:T(8,128)S(1)} %get-tuple-element.380, f32[32,4,4,8]{0,3,1,2:T(8,128)S(1)} %max.5, pred[32,512]{1,0:T(8,128)(4,1)S(1)} %bitcast.76), kind=kLoop, calls=%fused_computation.5 | loop fusion | flops 10481664 | bytes 12632064 | tf_op jit(solution)/shard_map/while/body/eval_jaxpr/cond/branch_1_fun/convert_element_type | solution.py:66
  141.9 0.1 copy.53
  142.0 6.9 %bitcast_add_fusion = f32[32,4,4,8,128]{4,3,1,0,2:T(8,128)} fusion(f32[32,4,4,8,128]{4,3,1,0,2:T(8,128)} %get-tuple-element.307, bf16[512,4,128,1,1]{0,2,4,3,1:T(8,128)(2,1)S(1)} %bitcast.71, bf16[32,4,4,8,512]{4,0,3,1,2:T(8,128)(2,1)} %get-tuple-element.377, f32[32,4,4,8]{3,1,0,2:T(4,128)S(1)} %copy.53), kind=kOutput, calls=%fused_computation.9 | convolution fusion | flops 537919488 | bytes 8929280 | tf_op jit(solution)/shard_map/while/body/eval_jaxpr/cond/branch_1_fun/rtjgn,njd->rtjgd/dot_general | solution.py:64
  148.9 0.7 fusion.35
  150.3 13.6 %conditional.2 = ((f32[32,4,4,8]{0,3,1,2:T(8,128)S(1)}, f32[32,4,4,8]{0,3,1,2:T(8,128)S(1)}, f32[32,4,4,8,128]{4,3,1,0,2:T(8,128)})) conditional(s32[]{:T(128)} %convert_element_type.51, (f32[32,4,4,8]{0,3,1,2:T(8,128)S(1)}, f32[32,4,4,8]{0,3,1,2:T(8,128)S(1)}, f32[32,4,4,8,128]{4,3,1,0,2:T(8,128)}) %tuple.66, (pred[32,4]{1,0:T(8,128)(4,1)S(1)}, ...), branch_computations={%region_6.6_spmd, %region_7.9_spmd} | conditional | flops 1091575808 | bytes 33915068 | solution.py:89
  150.4 1.3 constant_dynamic-slice_fusion
  151.8 1.3 fusion
  153.1 3.7 %fusion.3 = (bf16[32,4,4,8,512]{4,0,3,1,2:T(8,128)(2,1)}, f32[32,4,4,8]{0,3,1,2:T(8,128)S(1)}) fusion(f32[4,512,32,4,8]{1,2,4,3,0:T(8,128)S(1)} %get-tuple-element.380, f32[32,4,4,8]{0,3,1,2:T(8,128)S(1)} %max.5, pred[32,512]{1,0:T(8,128)(4,1)S(1)} %bitcast.76), kind=kLoop, calls=%fused_computation.5 | loop fusion | flops 10481664 | bytes 12632064 | tf_op jit(solution)/shard_map/while/body/eval_jaxpr/cond/branch_1_fun/convert_element_type | solution.py:66
  157.0 6.9 %bitcast_add_fusion = f32[32,4,4,8,128]{4,3,1,0,2:T(8,128)} fusion(f32[32,4,4,8,128]{4,3,1,0,2:T(8,128)} %get-tuple-element.307, bf16[512,4,128,1,1]{0,2,4,3,1:T(8,128)(2,1)S(1)} %bitcast.71, bf16[32,4,4,8,512]{4,0,3,1,2:T(8,128)(2,1)} %get-tuple-element.377, f32[32,4,4,8]{3,1,0,2:T(4,128)S(1)} %copy.53), kind=kOutput, calls=%fused_computation.9 | convolution fusion | flops 537919488 | bytes 8929280 | tf_op jit(solution)/shard_map/while/body/eval_jaxpr/cond/branch_1_fun/rtjgn,njd->rtjgd/dot_general | solution.py:64
  164.1 1.9 divide_convert_fusion
  166.0 0.3 copy.68
  166.3 0.8 convolution_convert_fusion
  167.1 1.6 copy.69
  168.8 51.5 %all_to_all.5 = bf16[8,8,4,4096]{3,2,1,0:T(4,128)(2,1)S(1)} all-to-all(bf16[8,8,4,4096]{3,2,1,0:T(4,128)(2,1)S(1)} %copy.69), channel_id=1, replica_groups=mesh['groups'=2,'ctx'=4,'head'=2,'row'=2] {'ctx','row'}, dimensions={0} | all-to-all | bytes 4194304 | tf_op jit(solution)/shard_map/all_to_all | solution.py:153
  220.3 1.3 copy.120
  (52 shorter events, 1.7 us)
Async XLA Ops:
  6.5 12.8 %copy-start = (bf16[32,4,512]{2,1,0:T(4,128)(2,1)S(1)}, bf16[32,4,512]{2,1,0:T(4,128)(2,1)}, u32[]{:S(2)}) copy-start(bf16[32,4,512]{2,1,0:T(4,128)(2,1)} %param.14) | copy-start | bytes 393220
  6.5 4.3 %copy-start.2 = (bf16[32,4,4096]{2,1,0:T(4,128)(2,1)S(1)}, bf16[32,4,4096]{2,1,0:T(4,128)(2,1)}, u32[]{:S(2)}) copy-start(bf16[32,4,4096]{2,1,0:T(4,128)(2,1)} %param.12) | copy-start | bytes 3145732
  6.5 51.1 %all-gather.3.cloned.1.call-start = ((), (), s32[]{:S(2)}) async-start(), calls=%async_computation.1 | async-start | bytes 2621440 | tf_op jit(solution)/shard_map/all_gather | solution.py:132
  8.7 95.2 %all-gather.5.cloned.1.call-start = ((), (), s32[]{:S(2)}) async-start(), calls=%async_computation.2 | async-start | bytes 2621440 | tf_op jit(solution)/shard_map/all_gather | solution.py:133
  10.8 1.8 copy-start.5
  21.0 1.5 copy-start.1
  21.0 2.8 %copy-start.3 = (s32[32,8]{0,1:T(8,128)S(1)}, s32[32,8]{0,1:T(8,128)}, u32[]{:S(2)}) copy-start(s32[32,8]{0,1:T(8,128)} %param.17) | copy-start | bytes 3076
  21.0 2.9 %copy-start.6 = (s32[32,1]{0,1:T(1,128)S(1)}, s32[32,1]{0,1:T(1,128)}, u32[]{:S(2)}) copy-start(s32[32,1]{0,1:T(1,128)} %param.19) | copy-start | bytes 388
  21.0 3.1 %copy-start.4 = (s32[32]{0:T(128)S(1)}, s32[32]{0:T(128)}, u32[]{:S(2)}) copy-start(s32[32]{0:T(128)} %param.18) | copy-start | bytes 388
Sparse Core Ops, SparseCore 0:
  8.9 48.6 all-gather.2
  59.2 44.6 all-gather.4
where the time goes:
time: 229 us; the launch traced here: 228 us
  waiting for transfers between devices  79.5 us (35%)
  blocking collectives  51.5 us (22%)
  matrix products  41 us (18%)
  other arithmetic  21.2 us (9%)
  local copies, waits for them, and re-layouts  18.8 us (8%)
  between operations  13.6 us (6%)
  loops' own time  2.78 us (1%)
    all_to_all x1, blocking collectives, body(): lax.all_to_all(outbox, ('ctx', 'row'), split_axis=0, concat_axis=0, tiled...  51.5 us
    all_gather x1, waiting for transfers between devices, body(): lax.all_gather(prefix_page_values, 'ctx', axis=0, tiled=True)  46.3 us
    all_gather x1, waiting for transfers between devices, body(): lax.all_gather(prefix_page_keys, 'ctx', axis=0, tiled=True)  33.3 us
    dot_general x4, matrix products, attend_block(): jnp.einsum('rtjgn,njd->rtjgd', weights.astype(jnp.bfloat16), values_blk,...  27.5 us
    convert_element_type x4, other arithmetic, attend_block(): weights.astype(jnp.bfloat16)  14.8 us
    unnamed x17, local copies, waits for them, and re-layouts  5.55 us
    dot_general x1, matrix products, causal_state(): jnp.einsum('rtjgd,rujd->rtjgu', grouped_heads, fresh_keys, preferred_elem...  5.49 us
    dot_general x4, matrix products, attend_block(): jnp.einsum('rtjgd,njd->rtjgn', grouped_heads, keys_blk, preferred_element...  5.38 us
  transfers between devices with their start and end apart: 2, of which 2 were waited for; matrix products, arithmetic and copies ran while one was open for 7% of the time, Pallas kernels for 0%

commit v1 on v0

v1 whole, which is shorter than its diff:
```python
import functools

import jax
import jax.numpy as jnp
from jax import lax
from jax.experimental import pallas as pl
from jax.experimental.pallas import tpu as pltpu
from jax.sharding import PartitionSpec as P

HEAD_SIZE = 128
PAGE_TOKENS = 128
BLOCK_ROWS = 8
LOWEST = -1e30
STACK = 2
MESH = pl.DeviceIdType.MESH


def kernel(
    dims,
    len_ref,
    home_ref,
    pages_ref,
    q_ref,
    nk_ref,
    nv_ref,
    pk_ref,
    pv_ref,
    out_ref,
    kv,
    bias,
    own_bias,
    scores,
    own_scores,
    placing,
    outbox,
    load_sem,
    up_send,
    down_send,
    z_recv,
    mate_send,
    mate_recv,
    out_send,
    out_recv,
    own_sem,
):
    ctx, steps, cap, kv_heads, per_key = dims
    rows4 = q_ref.shape[0]
    rows = rows4 // steps
    owners = 2 * ctx
    half = kv.shape[4]
    slots = pages_ref.shape[1]
    pool = ctx * 2 * half // PAGE_TOKENS
    wide = per_key * HEAD_SIZE
    pieces = 2 * ctx
    c = lax.axis_index("ctx")
    r = lax.axis_index("row")
    me = c * 2 + r
    factor = HEAD_SIZE ** (-0.5)

    def load(j, h, which):
        source = (pk_ref, pv_ref)[which]
        return pltpu.make_async_copy(
            source.at[pl.ds(h * half, half), pl.ds(j * HEAD_SIZE, HEAD_SIZE)],
            kv.at[j, c, h, which],
            load_sem.at[j, h, which],
        )

    for j in range(kv_heads):
        for h in range(2):
            for which in range(2):
                load(j, h, which).start()

    barrier = pltpu.get_barrier_semaphore()

    def greet(k, _):
        other = lax.rem(me + k, owners)
        pl.semaphore_signal(
            barrier,
            inc=1,
            device_id={"ctx": other // 2, "row": lax.rem(other, 2)},
            device_id_type=MESH,
        )
        return 0

    lax.fori_loop(1, owners, greet, 0)
    pl.semaphore_wait(barrier, owners - 1)

    def along(j, o, ahead):
        step = 1 if ahead else -1
        target = jnp.clip(c + step, 0, ctx - 1)
        return pltpu.make_async_remote_copy(
            src_ref=kv.at[j, o, r],
            dst_ref=kv.at[j, o, r],
            send_sem=(up_send if ahead else down_send).at[j, o],
            recv_sem=z_recv.at[j, o],
            device_id={"ctx": target, "row": r},
            device_id_type=MESH,
        )

    def across(j, o, h):
        return pltpu.make_async_remote_copy(
            src_ref=kv.at[j, o, h],
            dst_ref=kv.at[j, o, h],
            send_sem=mate_send.at[j, o],
            recv_sem=mate_recv.at[j, o],
            device_id={"ctx": c, "row": 1 - r},
            device_id_type=MESH,
        )

    def send_own(j):
        @pl.when(c < ctx - 1)
        def _():
            along(j, c, True).start()

        @pl.when(c > 0)
        def _():
            along(j, c, False).start()

    def relay(j, s):
        low, high = c - s, c + s

        @pl.when(low >= 0)
        def _():
            along(j, low, True).wait_recv()

            @pl.when(c < ctx - 1)
            def _():
                along(j, low, True).start()

            across(j, low, r).start()

        @pl.when(high < ctx)
        def _():
            along(j, high, False).wait_recv()

            @pl.when(c > 0)
            def _():
                along(j, high, False).start()

            across(j, high, r).start()

    def wait_mate(j):
        def one(k, _):
            o = lax.rem(c + k, ctx)
            across(j, o, 1 - r).wait_recv()
            return 0

        lax.fori_loop(1, ctx, one, 0)

    for j in range(kv_heads):
        for h in range(2):
            for which in range(2):
                load(j, h, which).wait()
        send_own(j)

    row_of = lax.broadcasted_iota(jnp.int32, (rows4, 1), 0) // steps
    lane_row = lax.broadcasted_iota(jnp.int32, (1, rows4), 1) // steps
    lane_step = lax.rem(lax.broadcasted_iota(jnp.int32, (1, rows4), 1), steps)
    length = jnp.zeros((rows4, 1), jnp.int32)
    home_col = jnp.zeros((rows4, 1), jnp.int32)
    home_lane = jnp.zeros((1, rows4), jnp.int32)
    for i in range(rows):
        length = jnp.where(row_of == i, len_ref[i], length)
        home_col = jnp.where(row_of == i, home_ref[i], home_col)
        home_lane = jnp.where(lane_row == i, home_ref[i], home_lane)

    page_id = lax.broadcasted_iota(jnp.int32, (rows4, pool), 1)
    used = jnp.zeros((rows4, pool), jnp.float32)
    block_of = row_of // BLOCK_ROWS
    first_block = me * (rows // BLOCK_ROWS)
    for slot in range(slots):
        page = jnp.zeros((rows4, 1), jnp.int32)
        for b in range(rows // BLOCK_ROWS):
            page = jnp.where(block_of == b, pages_ref[first_block + b, slot], page)
        page = jnp.where(slot < length, page, -1)
        used = jnp.where(page_id == page, 1.0, used)
    floor = jnp.where(used > 0.5, 0.0, LOWEST)
    per_piece = half // PAGE_TOKENS
    for p in range(pool):
        at = (p % per_piece) * PAGE_TOKENS
        bias[p // per_piece, :, at : at + PAGE_TOKENS] = jnp.broadcast_to(
            floor[:, p : p + 1], (rows4, PAGE_TOKENS)
        )
    row_step = lax.rem(lax.broadcasted_iota(jnp.int32, (rows4, 1), 0), steps)
    own_bias[...] = jnp.where((row_of == lane_row) & (lane_step <= row_step), 0.0, LOWEST)

    earlier = (home_col == home_lane) & (row_of < lane_row) & (row_step == 0)
    position = jnp.sum(jnp.where(earlier, 1.0, 0.0), axis=0, keepdims=True).astype(jnp.int32)
    target = (home_lane * cap + position) * steps + lane_step
    slot_row = lax.broadcasted_iota(jnp.int32, (owners * cap * steps, rows4), 0)
    placing[...] = jnp.where(slot_row == target, 1.0, 0.0).astype(jnp.bfloat16)

    def first(s, _):
        relay(0, s)
        return 0

    lax.fori_loop(1, ctx, first, 0)

    chunks = per_key // STACK
    relays = -(-(ctx - 1) // chunks)
    contract = (((1,), (1,)), ((), ()))

    def over_pieces(step, init):
        if pieces <= 8:
            state = init
            for i in range(pieces):
                state = step(i, i // 2, i % 2, state)
            return state
        return lax.fori_loop(0, pieces, lambda i, st: step(i, i // 2, lax.rem(i, 2), st), init)

    def fold(op, array):
        got = array[:, :HEAD_SIZE]
        for at in range(HEAD_SIZE, array.shape[1], HEAD_SIZE):
            got = op(got, array[:, at : at + HEAD_SIZE])
        return got

    def send_result(j, o):
        return pltpu.make_async_remote_copy(
            src_ref=outbox.at[j, o],
            dst_ref=out_ref.at[me, :, pl.ds(pl.multiple_of(j * wide, wide), wide)],
            send_sem=out_send.at[j, o],
            recv_sem=out_recv.at[j, me],
            device_id={"ctx": o // 2, "row": lax.rem(o, 2)},
            device_id_type=MESH,
        )

    def take_result(j, o):
        return pltpu.make_async_remote_copy(
            src_ref=outbox.at[j, o],
            dst_ref=out_ref.at[o, :, pl.ds(pl.multiple_of(j * wide, wide), wide)],
            send_sem=out_send.at[j, o],
            recv_sem=out_recv.at[j, o],
            device_id={"ctx": o // 2, "row": lax.rem(o, 2)},
            device_id_type=MESH,
        )

    def keep_result(j):
        return pltpu.make_async_copy(
            outbox.at[j, me],
            out_ref.at[me, :, pl.ds(pl.multiple_of(j * wide, wide), wide)],
            own_sem.at[j],
        )

    def one_head(j, _):
        wait_mate(j)
        head_at = pl.multiple_of(j * HEAD_SIZE, HEAD_SIZE)

        def one_chunk(k, _):
            @pl.when(j + 1 < kv_heads)
            def _():
                for i in range(relays):
                    s = k * relays + i + 1

                    @pl.when(s < ctx)
                    def _():
                        relay(j + 1, s)

            lead = (j * per_key + k * STACK) * HEAD_SIZE
            query = jnp.concatenate(
                [
                    q_ref[:, pl.ds(pl.multiple_of(lead + g * HEAD_SIZE, HEAD_SIZE), HEAD_SIZE)]
                    for g in range(STACK)
                ],
                axis=0,
            )
            own = (
                lax.dot_general(
                    query,
                    nk_ref[:, pl.ds(head_at, HEAD_SIZE)],
                    contract,
                    preferred_element_type=jnp.float32,
                )
                * factor
                + jnp.concatenate([own_bias[...]] * STACK, axis=0)
            )

            def score(i, o, h, peak):
                got = (
                    lax.dot_general(
                        query, kv[j, o, h, 0], contract, preferred_element_type=jnp.float32
                    )
                    * factor
                    + jnp.concatenate([bias[i]] * STACK, axis=0)
                )
                scores[i] = got
                return jnp.maximum(peak, fold(jnp.maximum, got))

            peak = jnp.max(over_pieces(score, own), axis=1, keepdims=True)
            weight = jnp.exp(own - peak)
            total = weight
            summed = jnp.dot(
                weight.astype(jnp.bfloat16),
                nv_ref[:, pl.ds(head_at, HEAD_SIZE)],
                preferred_element_type=jnp.float32,
            )

            def gather(i, o, h, state):
                total, summed = state
                weight = jnp.exp(scores[i] - peak)
                summed = summed + jnp.dot(
                    weight.astype(jnp.bfloat16), kv[j, o, h, 1], preferred_element_type=jnp.float32
                )
                return total + fold(jnp.add, weight), summed

            total, summed = over_pieces(gather, (total, summed))
            attended = (summed / jnp.sum(total, axis=1, keepdims=True)).astype(jnp.bfloat16)
            for g in range(STACK):
                placed = jnp.dot(
                    placing[...],
                    attended[g * rows4 : (g + 1) * rows4],
                    preferred_element_type=jnp.float32,
                )
                at = pl.multiple_of((k * STACK + g) * HEAD_SIZE, HEAD_SIZE)
                outbox[j, :, :, pl.ds(at, HEAD_SIZE)] = placed.reshape(
                    owners, cap * steps, HEAD_SIZE
                ).astype(jnp.bfloat16)
            return 0

        lax.fori_loop(0, chunks, one_chunk, 0)

        def deliver(k, _):
            send_result(j, lax.rem(me + k, owners)).start()
            return 0

        lax.fori_loop(1, owners, deliver, 0)
        keep_result(j).start()
        return 0

    lax.fori_loop(0, kv_heads, one_head, 0)

    def settle(j, _):
        keep_result(j).wait()

        def pages(k, _):
            o = lax.rem(c + k, ctx)
            across(j, o, r).wait_send()
            return 0

        lax.fori_loop(1, ctx, pages, 0)

        def hops(o, _):
            @pl.when((c < ctx - 1) & (o <= c))
            def _():
                along(j, o, True).wait_send()

            @pl.when((c > 0) & (o >= c))
            def _():
                along(j, o, False).wait_send()

            return 0

        lax.fori_loop(0, ctx, hops, 0)

        def results(k, _):
            o = lax.rem(me + k, owners)
            send_result(j, o).wait_send()
            take_result(j, o).wait_recv()
            return 0

        lax.fori_loop(1, owners, results, 0)
        return 0

    lax.fori_loop(0, kv_heads, settle, 0)


def body(
    queries,
    row_new_keys,
    row_new_values,
    prefix_page_keys,
    prefix_page_values,
    block_pages,
    row_len,
    home,
):
    rows, steps, width = queries.shape
    kv_heads = row_new_keys.shape[2] // HEAD_SIZE
    per_key = width // row_new_keys.shape[2]
    ctx = lax.axis_size("ctx")
    owners = ctx * lax.axis_size("row")
    cap = max(2, 2 * rows // owners)
    tokens = prefix_page_keys.shape[0]
    half = tokens // 2
    rows4 = rows * steps
    pieces = 2 * ctx
    stacked = STACK * rows4
    smem = pl.BlockSpec(memory_space=pltpu.SMEM)
    vmem = pl.BlockSpec(memory_space=pltpu.VMEM)
    hbm = pl.BlockSpec(memory_space=pl.ANY)
    dma = pltpu.SemaphoreType.DMA
    flops = 4 * rows4 * width * (tokens * ctx + rows4)
    out = pl.pallas_call(
        functools.partial(kernel, (ctx, steps, cap, kv_heads, per_key)),
        out_shape=jax.ShapeDtypeStruct((owners, cap * steps, width), jnp.bfloat16),
        in_specs=[smem, smem, smem, vmem, vmem, vmem, hbm, hbm],
        out_specs=hbm,
        scratch_shapes=[
            pltpu.VMEM((kv_heads, ctx, 2, 2, half, HEAD_SIZE), jnp.bfloat16),
            pltpu.VMEM((pieces, rows4, half), jnp.float32),
            pltpu.VMEM((rows4, rows4), jnp.float32),
            pltpu.VMEM((pieces, stacked, half), jnp.float32),
            pltpu.VMEM((stacked, rows4), jnp.float32),
            pltpu.VMEM((owners * cap * steps, rows4), jnp.bfloat16),
            pltpu.VMEM((kv_heads, owners, cap * steps, per_key * HEAD_SIZE), jnp.bfloat16),
            dma((kv_heads, 2, 2)),
            dma((kv_heads, ctx)),
            dma((kv_heads, ctx)),
            dma((kv_heads, ctx)),
            dma((kv_heads, ctx)),
            dma((kv_heads, ctx)),
            dma((kv_heads, owners)),
            dma((kv_heads, owners)),
            dma((kv_heads,)),
        ],
        compiler_params=pltpu.CompilerParams(
            collective_id=0, has_side_effects=True, vmem_limit_bytes=48 * 1024 * 1024
        ),
        cost_estimate=pl.CostEstimate(
            flops=flops, bytes_accessed=8 * 1024 * 1024, transcendentals=flops // 512
        ),
    )(
        row_len,
        home[:, 0],
        block_pages,
        queries.reshape(rows4, width),
        row_new_keys.reshape(rows4, -1),
        row_new_values.reshape(rows4, -1),
        prefix_page_keys,
        prefix_page_values,
    )
    return out.reshape(1, owners, cap, steps, width)


def solution(mesh):
    return jax.shard_map(
        body,
        mesh=mesh,
        in_specs=(
            P(("groups", "ctx", "row"), None, "head"),
            P(("groups", "ctx", "row"), None, "head"),
            P(("groups", "ctx", "row"), None, "head"),
            P(("groups", "ctx"), "head"),
            P(("groups", "ctx"), "head"),
            P("groups", None),
            P(("groups", "ctx", "row")),
            P(("groups", "ctx", "row"), None),
        ),
        out_specs=P(("groups", "ctx", "row"), None, None, None, "head"),
        check_vma=False,
    )
```

time: 229 us -> 103 us (0.45)
  Pallas kernels: 0 us -> 94.1 us
  waiting for transfers between devices: 79.5 us -> 0 us
  blocking collectives: 51.5 us -> 0 us
  matrix products: 41 us -> 0 us
  other arithmetic: 21.2 us -> 0 us
  between operations: 13.6 us -> 0.05 us
  local copies, waits for them, and re-layouts: 18.8 us -> 8.3 us
  loops' own time: 2.78 us -> 0 us
    pallas_call x0 -> x1, Pallas kernels: none -> 94.1 us  [body(): pl.pallas_call(functools.partial(kernel, (ctx, steps, cap, kv_heads, per_...]
    all_gather x2 -> x0, waiting for transfers between devices: 79.5 us -> none  [the longest x1 46.3 us: body(): lax.all_gather(prefix_page_values, 'ctx', axis=0, tiled=True)]
    all_to_all x1 -> x0, blocking collectives: 51.5 us -> none  [body(): lax.all_to_all(outbox, ('ctx', 'row'), split_axis=0, concat_axis=0, tiled...]
    dot_general x12 -> x0, matrix products: 41 us -> none  [the longest x4 27.5 us: attend_block(): jnp.einsum('rtjgn,njd->rtjgd', weights.astype(jnp.bfloat16), values_blk,...]
    convert_element_type x6 -> x0, other arithmetic: 16.8 us -> none  [the longest x4 14.8 us: attend_block(): weights.astype(jnp.bfloat16)]
    dynamic_slice x8 -> x0, local copies, waits for them, and re-layouts: 5.53 us -> none  [the longest x4 5.11 us: advance(): lax.dynamic_slice_in_dim(page_v, offset, block_len, 0)]
    while x5 -> x0, local copies, waits for them, and re-layouts: 3.59 us -> none  [fold_pages(): return lax.fori_loop(0, token_count // block_len, advance, running)]
    reduce_or x4 -> x0, other arithmetic: 2.81 us -> none  [advance(): jnp.any(mask_pages)]
  transfers between devices with their start and end apart: 2 -> 0, of which waited for: 2 -> 0; matrix products, arithmetic and copies ran while one was open for 7% -> 0% of each run, Pallas kernels for 0% -> 0%
where the time goes in v1:
time: 103 us; the launch traced here: 102 us
  Pallas kernels  94.1 us (91%)
  local copies, waits for them, and re-layouts  8.3 us (8%)
    pallas_call x1, Pallas kernels, body(): pl.pallas_call(functools.partial(kernel, (ctx, steps, cap, kv_heads, per_...  94.1 us
    unnamed x9, local copies, waits for them, and re-layouts  2.87 us
    reshape x1, local copies, waits for them, and re-layouts, body(): return out.reshape(1, owners, cap, steps, width)  2.2 us

profile of v1, /device:TPU:0, one launch (start us, length us, event | category | flops | bytes accessed | tf_op | source)
XLA Modules:
  0.0 102.4 jit_solution(10582865313375665941)
XLA Ops:
  0.0 0.0 copy-start.3
  0.0 0.0 copy-start.2
  0.0 0.8 copy.9.pages_ref
  0.8 0.9 reshape.13.nk_ref
  1.7 0.9 reshape.14.nv_ref
  2.7 1.3 %reshape.12.q_ref = bf16[128,4096]{1,0:T(8,128)(2,1)S(1)} reshape(bf16[32,4,4096]{2,1,0:T(4,128)(2,1)} %param.8) | data formatting | bytes 2097152 | tf_op jit(solution)/shard_map/reshape | solution.py:425
  4.0 0.0 copy-done.3
  4.0 0.0 copy-done.2
  4.1 0.0 copy-start
  4.1 1.0 %copy-done = bf16[512,512]{1,0:T(8,128)(2,1)S(1)} copy-done((bf16[512,512]{1,0:T(8,128)(2,1)S(1)}, bf16[512,512]{1,0:T(8,128)(2,1)}, u32[]{:S(2)}) %copy-start) | copy-done | bytes 524312
  5.1 0.0 copy-start.1
  5.1 1.0 %copy-done.1 = bf16[512,512]{1,0:T(8,128)(2,1)S(1)} copy-done((bf16[512,512]{1,0:T(8,128)(2,1)S(1)}, bf16[512,512]{1,0:T(8,128)(2,1)}, u32[]{:S(2)}) %copy-start.1) | copy-done | bytes 524312
  6.1 94.1 %shard_map.82 = bf16[8,32,4096]{2,1,0:T(8,128)(2,1)S(1)} custom-call(s32[32]{0:T(128)S(1)} %copy-done.2, s32[32]{0:T(128)S(1)} %bitcast.1, s32[32,8]{1,0:T(8,128)S(1)} %copy.9.pages_ref, bf16[128,4096]{1,0:T(8,128)(2,1)S(1)} %reshape.12.q_ref, bf16[128,512]{1,0:T(8,128)(2,1)S(1)} %reshape.13.nk_ref, bf16[128,512]{1,0:T(8,128)(2,1)S(1)} %reshape.14.nv_ref, ...), custom_call_target="tpu_custom_call" | custom-call | flops 4563402752 | bytes 8388608 | tf_op jit(solution)/shard_map/pallas_call | solution.py:392
  100.2 2.2 %reshape.15 = bf16[1,8,8,4,4096]{4,3,2,1,0:T(4,128)(2,1)} reshape(bf16[8,32,4096]{2,1,0:T(8,128)(2,1)S(1)} %shard_map.82) | data formatting | bytes 4194304 | tf_op jit(solution)/shard_map/reshape | solution.py:431
Async XLA Ops:
  0.0 4.0 %copy-start.3 = (s32[32,1]{0,1:T(1,128)S(1)}, s32[32,1]{0,1:T(1,128)}, u32[]{:S(2)}) copy-start(s32[32,1]{0,1:T(1,128)} %param.15) | copy-start | bytes 388
  0.0 4.0 %copy-start.2 = (s32[32]{0:T(128)S(1)}, s32[32]{0:T(128)}, u32[]{:S(2)}) copy-start(s32[32]{0:T(128)} %len_ref.1) | copy-start | bytes 388
  4.1 1.0 %copy-start = (bf16[512,512]{1,0:T(8,128)(2,1)S(1)}, bf16[512,512]{1,0:T(8,128)(2,1)}, u32[]{:S(2)}) copy-start(bf16[512,512]{1,0:T(8,128)(2,1)} %pk_ref.1) | copy-start | bytes 1572868
  5.1 1.0 %copy-start.1 = (bf16[512,512]{1,0:T(8,128)(2,1)S(1)}, bf16[512,512]{1,0:T(8,128)(2,1)}, u32[]{:S(2)}) copy-start(bf16[512,512]{1,0:T(8,128)(2,1)} %pv_ref.1) | copy-start | bytes 1572868

commit v2 on v1

--- a/solution.py
+++ b/solution.py
@@ -10,8 +10,10 @@
 HEAD_SIZE = 128
 PAGE_TOKENS = 128
 BLOCK_ROWS = 8
+VMEM_BYTES = 58 * 1024 * 1024
 LOWEST = -1e30
 STACK = 2
+AHEAD = 2
 MESH = pl.DeviceIdType.MESH
 
 
@@ -20,17 +22,23 @@
     len_ref,
     home_ref,
     pages_ref,
+    q_hbm,
+    nk_hbm,
+    nv_hbm,
+    pk_ref,
+    pv_ref,
+    out_ref,
     q_ref,
     nk_ref,
     nv_ref,
-    pk_ref,
-    pv_ref,
-    out_ref,
+    row_sem,
+    q_flat,
+    nk_flat,
+    nv_flat,
     kv,
     bias,
     own_bias,
     scores,
-    own_scores,
     placing,
     outbox,
     load_sem,
@@ -44,11 +52,11 @@
     own_sem,
 ):
     ctx, steps, cap, kv_heads, per_key = dims
-    rows4 = q_ref.shape[0]
-    rows = rows4 // steps
+    rows = q_ref.shape[0]
+    rows4 = rows * steps
     owners = 2 * ctx
     half = kv.shape[4]
-    slots = pages_ref.shape[1]
+    slots = pages_ref.shape[0]
     pool = ctx * 2 * half // PAGE_TOKENS
     wide = per_key * HEAD_SIZE
     pieces = 2 * ctx
@@ -69,6 +77,14 @@
         for h in range(2):
             for which in range(2):
                 load(j, h, which).start()
+    own_rows = [
+        pltpu.make_async_copy(source, target, row_sem.at[i])
+        for i, (source, target) in enumerate(
+            ((q_hbm, q_ref), (nk_hbm, nk_ref), (nv_hbm, nv_ref))
+        )
+    ]
+    for copy in own_rows:
+        copy.start()
 
     barrier = pltpu.get_barrier_semaphore()
 
@@ -151,7 +167,9 @@
         for h in range(2):
             for which in range(2):
                 load(j, h, which).wait()
-        send_own(j)
+        if j < AHEAD:
+            send_own(j)
+    relay(0, 1)
 
     row_of = lax.broadcasted_iota(jnp.int32, (rows4, 1), 0) // steps
     lane_row = lax.broadcasted_iota(jnp.int32, (1, rows4), 1) // steps
@@ -171,7 +189,7 @@
     for slot in range(slots):
         page = jnp.zeros((rows4, 1), jnp.int32)
         for b in range(rows // BLOCK_ROWS):
-            page = jnp.where(block_of == b, pages_ref[first_block + b, slot], page)
+            page = jnp.where(block_of == b, pages_ref[slot, first_block + b], page)
         page = jnp.where(slot < length, page, -1)
         used = jnp.where(page_id == page, 1.0, used)
     floor = jnp.where(used > 0.5, 0.0, LOWEST)
@@ -190,11 +208,28 @@
     slot_row = lax.broadcasted_iota(jnp.int32, (owners * cap * steps, rows4), 0)
     placing[...] = jnp.where(slot_row == target, 1.0, 0.0).astype(jnp.bfloat16)
 
+    def flatten(source, target, h):
+        at = pl.multiple_of(h * HEAD_SIZE, HEAD_SIZE)
+        got = source[:, :, pl.ds(at, HEAD_SIZE)].astype(jnp.float32)
+        target[h] = got.reshape(rows4, HEAD_SIZE).astype(jnp.bfloat16)
+
+    for copy in own_rows:
+        copy.wait()
+
+    def flatten_queries(h, _):
+        flatten(q_ref, q_flat, h)
+        return 0
+
+    lax.fori_loop(0, kv_heads * per_key, flatten_queries, 0)
+    for j in range(kv_heads):
+        flatten(nk_ref, nk_flat, j)
+        flatten(nv_ref, nv_flat, j)
+
     def first(s, _):
         relay(0, s)
         return 0
 
-    lax.fori_loop(1, ctx, first, 0)
+    lax.fori_loop(2, ctx, first, 0)
 
     chunks = per_key // STACK
     relays = -(-(ctx - 1) // chunks)
@@ -242,8 +277,11 @@
         )
 
     def one_head(j, _):
+        @pl.when(j + AHEAD < kv_heads)
+        def _():
+            send_own(j + AHEAD)
+
         wait_mate(j)
-        head_at = pl.multiple_of(j * HEAD_SIZE, HEAD_SIZE)
 
         def one_chunk(k, _):
             @pl.when(j + 1 < kv_heads)
@@ -255,18 +293,12 @@
                     def _():
                         relay(j + 1, s)
 
-            lead = (j * per_key + k * STACK) * HEAD_SIZE
-            query = jnp.concatenate(
-                [
-                    q_ref[:, pl.ds(pl.multiple_of(lead + g * HEAD_SIZE, HEAD_SIZE), HEAD_SIZE)]
-                    for g in range(STACK)
-                ],
-                axis=0,
-            )
+            lead = j * per_key + k * STACK
+            query = q_flat[pl.ds(lead, STACK)].reshape(STACK * rows4, HEAD_SIZE)
             own = (
                 lax.dot_general(
                     query,
-                    nk_ref[:, pl.ds(head_at, HEAD_SIZE)],
+                    nk_flat[j],
                     contract,
                     preferred_element_type=jnp.float32,
                 )
@@ -290,7 +322,7 @@
             total = weight
             summed = jnp.dot(
                 weight.astype(jnp.bfloat16),
-                nv_ref[:, pl.ds(head_at, HEAD_SIZE)],
+                nv_flat[j],
                 preferred_element_type=jnp.float32,
             )
 
@@ -318,12 +350,27 @@
 
         lax.fori_loop(0, chunks, one_chunk, 0)
 
-        def deliver(k, _):
-            send_result(j, lax.rem(me + k, owners)).start()
+        def deliver(i, inner, k, _):
+            o = lax.rem(me + k, owners)
+            place = o // 2
+            middle = (place >= (ctx + 2) // 4) & (place < ctx - (ctx + 2) // 4)
+
+            @pl.when(middle if inner else ~middle)
+            def _():
+                send_result(i, o).start()
+
             return 0
 
-        lax.fori_loop(1, owners, deliver, 0)
         keep_result(j).start()
+        lax.fori_loop(1, owners, functools.partial(deliver, j, True), 0)
+
+        @pl.when(j >= kv_heads - 2)
+        def _():
+            def late(i, _):
+                return lax.fori_loop(1, owners, functools.partial(deliver, i, False), 0)
+
+            lax.fori_loop(jnp.where(j == kv_heads - 1, j, 0), j + 1, late, 0)
+
         return 0
 
     lax.fori_loop(0, kv_heads, one_head, 0)
@@ -385,21 +432,26 @@
     pieces = 2 * ctx
     stacked = STACK * rows4
     smem = pl.BlockSpec(memory_space=pltpu.SMEM)
-    vmem = pl.BlockSpec(memory_space=pltpu.VMEM)
     hbm = pl.BlockSpec(memory_space=pl.ANY)
     dma = pltpu.SemaphoreType.DMA
     flops = 4 * rows4 * width * (tokens * ctx + rows4)
     out = pl.pallas_call(
         functools.partial(kernel, (ctx, steps, cap, kv_heads, per_key)),
         out_shape=jax.ShapeDtypeStruct((owners, cap * steps, width), jnp.bfloat16),
-        in_specs=[smem, smem, smem, vmem, vmem, vmem, hbm, hbm],
+        in_specs=[smem, smem, smem, hbm, hbm, hbm, hbm, hbm],
         out_specs=hbm,
         scratch_shapes=[
+            pltpu.VMEM(queries.shape, jnp.bfloat16),
+            pltpu.VMEM(row_new_keys.shape, jnp.bfloat16),
+            pltpu.VMEM(row_new_values.shape, jnp.bfloat16),
+            dma((3,)),
+            pltpu.VMEM((kv_heads * per_key, rows4, HEAD_SIZE), jnp.bfloat16),
+            pltpu.VMEM((kv_heads, rows4, HEAD_SIZE), jnp.bfloat16),
+            pltpu.VMEM((kv_heads, rows4, HEAD_SIZE), jnp.bfloat16),
             pltpu.VMEM((kv_heads, ctx, 2, 2, half, HEAD_SIZE), jnp.bfloat16),
             pltpu.VMEM((pieces, rows4, half), jnp.float32),
             pltpu.VMEM((rows4, rows4), jnp.float32),
             pltpu.VMEM((pieces, stacked, half), jnp.float32),
-            pltpu.VMEM((stacked, rows4), jnp.float32),
             pltpu.VMEM((owners * cap * steps, rows4), jnp.bfloat16),
             pltpu.VMEM((kv_heads, owners, cap * steps, per_key * HEAD_SIZE), jnp.bfloat16),
             dma((kv_heads, 2, 2)),
@@ -413,7 +465,7 @@
             dma((kv_heads,)),
         ],
         compiler_params=pltpu.CompilerParams(
-            collective_id=0, has_side_effects=True, vmem_limit_bytes=48 * 1024 * 1024
+            collective_id=0, has_side_effects=True, vmem_limit_bytes=VMEM_BYTES
         ),
         cost_estimate=pl.CostEstimate(
             flops=flops, bytes_accessed=8 * 1024 * 1024, transcendentals=flops // 512
@@ -421,10 +473,10 @@
     )(
         row_len,
         home[:, 0],
-        block_pages,
-        queries.reshape(rows4, width),
-        row_new_keys.reshape(rows4, -1),
-        row_new_values.reshape(rows4, -1),
+        block_pages.T,
+        queries,
+        row_new_keys,
+        row_new_values,
         prefix_page_keys,
         prefix_page_values,
     )

time: 103 us -> 92.9 us (0.902)
  Pallas kernels: 94.1 us -> 87.8 us
  local copies, waits for them, and re-layouts: 8.3 us -> 4.1 us
    pallas_call x1, Pallas kernels: 94.1 us -> 87.8 us  [body(): pl.pallas_call(functools.partial(kernel, (ctx, steps, cap, kv_heads, per_...]
    reshape x3 -> x0, local copies, waits for them, and re-layouts: 3.22 us -> none  [the longest x1 1.34 us: body(): queries.reshape(rows4, width)]
    unnamed x9 -> x0, local copies, waits for them, and re-layouts: 2.87 us -> none
    reshape x1, local copies, waits for them, and re-layouts: 2.2 us -> 4.1 us  [body(): return out.reshape(1, owners, cap, steps, width)]
where the time goes in v2:
time: 92.9 us; the launch traced here: 91.9 us
  Pallas kernels  87.8 us (95%)
  local copies, waits for them, and re-layouts  4.1 us (4%)
    pallas_call x1, Pallas kernels, body(): pl.pallas_call(functools.partial(kernel, (ctx, steps, cap, kv_heads, per_...  87.8 us
    reshape x1, local copies, waits for them, and re-layouts, body(): return out.reshape(1, owners, cap, steps, width)  4.1 us

profile of v2, /device:TPU:0, one launch (start us, length us, event | category | flops | bytes accessed | tf_op | source)
XLA Modules:
  0.0 91.9 jit_solution(15721200501539663666)
XLA Ops:
  0.0 87.8 %shard_map.82 = bf16[8,32,4096]{2,1,0:T(8,128)(2,1)} custom-call(s32[32]{0:T(128)} %len_ref.1, s32[32]{0:T(128)} %bitcast.3, s32[8,32]{1,0:T(8,128)} %bitcast.2, bf16[32,4,4096]{2,1,0:T(4,128)(2,1)} %q_hbm.1, bf16[32,4,512]{2,1,0:T(4,128)(2,1)} %nk_hbm.1, bf16[32,4,512]{2,1,0:T(4,128)(2,1)} %nv_hbm.1, bf16[512,512]{1,0:T(8,128)(2,1)} %pk_ref.1, ...), custom_call_target="tpu_custom_call" | custom-call | flops 4563402752 | bytes 8388608 | tf_op jit(solution)/shard_map/pallas_call | solution.py:438
  87.8 4.1 %reshape.3 = bf16[1,8,8,4,4096]{4,3,2,1,0:T(4,128)(2,1)} reshape(bf16[8,32,4096]{2,1,0:T(8,128)(2,1)} %shard_map.82) | data formatting | bytes 4194304 | tf_op jit(solution)/shard_map/reshape | solution.py:483

commit v3 on v2

--- a/solution.py
+++ b/solution.py
@@ -12,8 +12,9 @@
 BLOCK_ROWS = 8
 VMEM_BYTES = 58 * 1024 * 1024
 LOWEST = -1e30
-STACK = 2
-AHEAD = 2
+PASSED = 2
+STACK = 4
+AHEAD = 3
 MESH = pl.DeviceIdType.MESH
 
 
@@ -167,9 +168,8 @@
         for h in range(2):
             for which in range(2):
                 load(j, h, which).wait()
-        if j < AHEAD:
+        if j < PASSED:
             send_own(j)
-    relay(0, 1)
 
     row_of = lax.broadcasted_iota(jnp.int32, (rows4, 1), 0) // steps
     lane_row = lax.broadcasted_iota(jnp.int32, (1, rows4), 1) // steps
@@ -208,6 +208,12 @@
     slot_row = lax.broadcasted_iota(jnp.int32, (owners * cap * steps, rows4), 0)
     placing[...] = jnp.where(slot_row == target, 1.0, 0.0).astype(jnp.bfloat16)
 
+    relay(0, 1)
+    for j in range(PASSED, AHEAD):
+        send_own(j)
+    for j in range(1, PASSED):
+        relay(j, 1)
+
     def flatten(source, target, h):
         at = pl.multiple_of(h * HEAD_SIZE, HEAD_SIZE)
         got = source[:, :, pl.ds(at, HEAD_SIZE)].astype(jnp.float32)
@@ -226,13 +232,14 @@
         flatten(nv_ref, nv_flat, j)
 
     def first(s, _):
-        relay(0, s)
+        for j in range(PASSED):
+            relay(j, s)
         return 0
 
     lax.fori_loop(2, ctx, first, 0)
 
     chunks = per_key // STACK
-    relays = -(-(ctx - 1) // chunks)
+    relays = -(-(ctx - 1) // (2 * chunks))
     contract = (((1,), (1,)), ((), ()))
 
     def over_pieces(step, init):
@@ -284,15 +291,17 @@
         wait_mate(j)
 
         def one_chunk(k, _):
-            @pl.when(j + 1 < kv_heads)
-            def _():
-                for i in range(relays):
-                    s = k * relays + i + 1
-
-                    @pl.when(s < ctx)
-                    def _():
-                        relay(j + 1, s)
-
+            def pass_on(turn):
+                @pl.when(j + PASSED < kv_heads)
+                def _():
+                    for i in range(relays):
+                        s = turn * relays + i + 1
+
+                        @pl.when(s < ctx)
+                        def _():
+                            relay(j + PASSED, s)
+
+            pass_on(2 * k)
             lead = j * per_key + k * STACK
             query = q_flat[pl.ds(lead, STACK)].reshape(STACK * rows4, HEAD_SIZE)
             own = (
@@ -318,6 +327,7 @@
                 return jnp.maximum(peak, fold(jnp.maximum, got))
 
             peak = jnp.max(over_pieces(score, own), axis=1, keepdims=True)
+            pass_on(2 * k + 1)
             weight = jnp.exp(own - peak)
             total = weight
             summed = jnp.dot(
@@ -350,27 +360,12 @@
 
         lax.fori_loop(0, chunks, one_chunk, 0)
 
-        def deliver(i, inner, k, _):
-            o = lax.rem(me + k, owners)
-            place = o // 2
-            middle = (place >= (ctx + 2) // 4) & (place < ctx - (ctx + 2) // 4)
-
-            @pl.when(middle if inner else ~middle)
-            def _():
-                send_result(i, o).start()
-
-            return 0
-
+        def deliver(k, _):
+            send_result(j, lax.rem(me + k, owners)).start()
+            return 0
+
+        lax.fori_loop(1, owners, deliver, 0)
         keep_result(j).start()
-        lax.fori_loop(1, owners, functools.partial(deliver, j, True), 0)
-
-        @pl.when(j >= kv_heads - 2)
-        def _():
-            def late(i, _):
-                return lax.fori_loop(1, owners, functools.partial(deliver, i, False), 0)
-
-            lax.fori_loop(jnp.where(j == kv_heads - 1, j, 0), j + 1, late, 0)
-
         return 0
 
     lax.fori_loop(0, kv_heads, one_head, 0)

time: 92.9 us -> 87.2 us (0.939)
  Pallas kernels: 87.8 us -> 82.9 us
    pallas_call x1, Pallas kernels: 87.8 us -> 82.9 us  [body(): pl.pallas_call(functools.partial(kernel, (ctx, steps, cap, kv_heads, per_...]
where the time goes in v3:
time: 87.2 us; the launch traced here: 87 us
  Pallas kernels  82.9 us (95%)
  local copies, waits for them, and re-layouts  4.1 us (5%)
    pallas_call x1, Pallas kernels, body(): pl.pallas_call(functools.partial(kernel, (ctx, steps, cap, kv_heads, per_...  82.9 us
    reshape x1, local copies, waits for them, and re-layouts, body(): return out.reshape(1, owners, cap, steps, width)  4.1 us

profile of v3, /device:TPU:0, one launch (start us, length us, event | category | flops | bytes accessed | tf_op | source)
XLA Modules:
  0.0 87.0 jit_solution(10463410994825952016)
XLA Ops:
  0.0 82.9 %shard_map.82 = bf16[8,32,4096]{2,1,0:T(8,128)(2,1)} custom-call(s32[32]{0:T(128)} %len_ref.1, s32[32]{0:T(128)} %bitcast.3, s32[8,32]{1,0:T(8,128)} %bitcast.2, bf16[32,4,4096]{2,1,0:T(4,128)(2,1)} %q_hbm.1, bf16[32,4,512]{2,1,0:T(4,128)(2,1)} %nk_hbm.1, bf16[32,4,512]{2,1,0:T(4,128)(2,1)} %nv_hbm.1, bf16[512,512]{1,0:T(8,128)(2,1)} %pk_ref.1, ...), custom_call_target="tpu_custom_call" | custom-call | flops 4563402752 | bytes 8388608 | tf_op jit(solution)/shard_map/pallas_call | solution.py:433
  82.9 4.1 %reshape.3 = bf16[1,8,8,4,4096]{4,3,2,1,0:T(4,128)(2,1)} reshape(bf16[8,32,4096]{2,1,0:T(8,128)(2,1)} %shard_map.82) | data formatting | bytes 4194304 | tf_op jit(solution)/shard_map/reshape | solution.py:478

commit v4 on v3

--- a/solution.py
+++ b/solution.py
@@ -59,7 +59,7 @@
     half = kv.shape[4]
     slots = pages_ref.shape[0]
     pool = ctx * 2 * half // PAGE_TOKENS
-    wide = per_key * HEAD_SIZE
+    wide = STACK * HEAD_SIZE
     pieces = 2 * ctx
     c = lax.axis_index("ctx")
     r = lax.axis_index("row")
@@ -346,33 +346,31 @@
 
             total, summed = over_pieces(gather, (total, summed))
             attended = (summed / jnp.sum(total, axis=1, keepdims=True)).astype(jnp.bfloat16)
+            part = j * chunks + k
             for g in range(STACK):
                 placed = jnp.dot(
                     placing[...],
                     attended[g * rows4 : (g + 1) * rows4],
                     preferred_element_type=jnp.float32,
                 )
-                at = pl.multiple_of((k * STACK + g) * HEAD_SIZE, HEAD_SIZE)
-                outbox[j, :, :, pl.ds(at, HEAD_SIZE)] = placed.reshape(
+                outbox[part, :, :, g * HEAD_SIZE : (g + 1) * HEAD_SIZE] = placed.reshape(
                     owners, cap * steps, HEAD_SIZE
                 ).astype(jnp.bfloat16)
+
+            def deliver(i, _):
+                send_result(part, lax.rem(me + i, owners)).start()
+                return 0
+
+            lax.fori_loop(1, owners, deliver, 0)
+            keep_result(part).start()
             return 0
 
         lax.fori_loop(0, chunks, one_chunk, 0)
-
-        def deliver(k, _):
-            send_result(j, lax.rem(me + k, owners)).start()
-            return 0
-
-        lax.fori_loop(1, owners, deliver, 0)
-        keep_result(j).start()
         return 0
 
     lax.fori_loop(0, kv_heads, one_head, 0)
 
     def settle(j, _):
-        keep_result(j).wait()
-
         def pages(k, _):
             o = lax.rem(c + k, ctx)
             across(j, o, r).wait_send()
@@ -393,16 +391,22 @@
 
         lax.fori_loop(0, ctx, hops, 0)
 
+        return 0
+
+    def settle_part(part, _):
+        keep_result(part).wait()
+
         def results(k, _):
             o = lax.rem(me + k, owners)
-            send_result(j, o).wait_send()
-            take_result(j, o).wait_recv()
+            send_result(part, o).wait_send()
+            take_result(part, o).wait_recv()
             return 0
 
         lax.fori_loop(1, owners, results, 0)
         return 0
 
     lax.fori_loop(0, kv_heads, settle, 0)
+    lax.fori_loop(0, kv_heads * chunks, settle_part, 0)
 
 
 def body(
@@ -424,6 +428,7 @@
     tokens = prefix_page_keys.shape[0]
     half = tokens // 2
     rows4 = rows * steps
+    parts = kv_heads * (per_key // STACK)
     pieces = 2 * ctx
     stacked = STACK * rows4
     smem = pl.BlockSpec(memory_space=pltpu.SMEM)
@@ -448,16 +453,16 @@
             pltpu.VMEM((rows4, rows4), jnp.float32),
             pltpu.VMEM((pieces, stacked, half), jnp.float32),
             pltpu.VMEM((owners * cap * steps, rows4), jnp.bfloat16),
-            pltpu.VMEM((kv_heads, owners, cap * steps, per_key * HEAD_SIZE), jnp.bfloat16),
+            pltpu.VMEM((parts, owners, cap * steps, STACK * HEAD_SIZE), jnp.bfloat16),
             dma((kv_heads, 2, 2)),
             dma((kv_heads, ctx)),
             dma((kv_heads, ctx)),
             dma((kv_heads, ctx)),
             dma((kv_heads, ctx)),
             dma((kv_heads, ctx)),
-            dma((kv_heads, owners)),
-            dma((kv_heads, owners)),
-            dma((kv_heads,)),
+            dma((parts, owners)),
+            dma((parts, owners)),
+            dma((parts,)),
         ],
         compiler_params=pltpu.CompilerParams(
             collective_id=0, has_side_effects=True, vmem_limit_bytes=VMEM_BYTES

time: 87.2 us -> 85.2 us (0.977)
  Pallas kernels: 82.9 us -> 80.9 us
    pallas_call x1, Pallas kernels: 82.9 us -> 80.9 us  [body(): pl.pallas_call(functools.partial(kernel, (ctx, steps, cap, kv_heads, per_...]
where the time goes in v4:
time: 85.2 us; the launch traced here: 85 us
  Pallas kernels  80.9 us (95%)
  local copies, waits for them, and re-layouts  4.1 us (5%)
    pallas_call x1, Pallas kernels, body(): pl.pallas_call(functools.partial(kernel, (ctx, steps, cap, kv_heads, per_...  80.9 us
    reshape x1, local copies, waits for them, and re-layouts, body(): return out.reshape(1, owners, cap, steps, width)  4.1 us

profile of v4, /device:TPU:0, one launch (start us, length us, event | category | flops | bytes accessed | tf_op | source)
XLA Modules:
  0.0 85.0 jit_solution(8714058736666346601)
XLA Ops:
  0.0 80.9 %shard_map.82 = bf16[8,32,4096]{2,1,0:T(8,128)(2,1)} custom-call(s32[32]{0:T(128)} %len_ref.1, s32[32]{0:T(128)} %bitcast.3, s32[8,32]{1,0:T(8,128)} %bitcast.2, bf16[32,4,4096]{2,1,0:T(4,128)(2,1)} %q_hbm.1, bf16[32,4,512]{2,1,0:T(4,128)(2,1)} %nk_hbm.1, bf16[32,4,512]{2,1,0:T(4,128)(2,1)} %nv_hbm.1, bf16[512,512]{1,0:T(8,128)(2,1)} %pk_ref.1, ...), custom_call_target="tpu_custom_call" | custom-call | flops 4563402752 | bytes 8388608 | tf_op jit(solution)/shard_map/pallas_call | solution.py:438
  80.9 4.1 %reshape.3 = bf16[1,8,8,4,4096]{4,3,2,1,0:T(4,128)(2,1)} reshape(bf16[8,32,4096]{2,1,0:T(8,128)(2,1)} %shard_map.82) | data formatting | bytes 4194304 | tf_op jit(solution)/shard_map/reshape | solution.py:483

commit v5 on v4

--- a/solution.py
+++ b/solution.py
@@ -13,7 +13,7 @@
 VMEM_BYTES = 58 * 1024 * 1024
 LOWEST = -1e30
 PASSED = 2
-STACK = 4
+STACK = 2
 AHEAD = 3
 MESH = pl.DeviceIdType.MESH
 

time: 85.2 us -> 86.2 us (1.012)
  Pallas kernels: 80.9 us -> 81.9 us
    pallas_call x1, Pallas kernels: 80.9 us -> 81.9 us  [body(): pl.pallas_call(functools.partial(kernel, (ctx, steps, cap, kv_heads, per_...]
where the time goes in v5:
time: 86.2 us; the launch traced here: 86 us
  Pallas kernels  81.9 us (95%)
  local copies, waits for them, and re-layouts  4.1 us (5%)
    pallas_call x1, Pallas kernels, body(): pl.pallas_call(functools.partial(kernel, (ctx, steps, cap, kv_heads, per_...  81.9 us
    reshape x1, local copies, waits for them, and re-layouts, body(): return out.reshape(1, owners, cap, steps, width)  4.1 us

profile of v5, /device:TPU:0, one launch (start us, length us, event | category | flops | bytes accessed | tf_op | source)
XLA Modules:
  0.0 86.0 jit_solution(577524308291892858)
XLA Ops:
  0.0 81.9 %shard_map.82 = bf16[8,32,4096]{2,1,0:T(8,128)(2,1)} custom-call(s32[32]{0:T(128)} %len_ref.1, s32[32]{0:T(128)} %bitcast.3, s32[8,32]{1,0:T(8,128)} %bitcast.2, bf16[32,4,4096]{2,1,0:T(4,128)(2,1)} %q_hbm.1, bf16[32,4,512]{2,1,0:T(4,128)(2,1)} %nk_hbm.1, bf16[32,4,512]{2,1,0:T(4,128)(2,1)} %nv_hbm.1, bf16[512,512]{1,0:T(8,128)(2,1)} %pk_ref.1, ...), custom_call_target="tpu_custom_call" | custom-call | flops 4563402752 | bytes 8388608 | tf_op jit(solution)/shard_map/pallas_call | solution.py:438
  81.9 4.1 %reshape.3 = bf16[1,8,8,4,4096]{4,3,2,1,0:T(4,128)(2,1)} reshape(bf16[8,32,4096]{2,1,0:T(8,128)(2,1)} %shard_map.82) | data formatting | bytes 4194304 | tf_op jit(solution)/shard_map/reshape | solution.py:483
